TPU v7x, 32 devices: a whole 2x2x4 slice. The times are simulated.
32 devices in a mesh: tank: 2 (over y), slab: 4 (over z), cross: 2 (over x), sub: 2 (over core).
Axes of the slice: x: 2, y: 2, z: 4, core: 2. Of those that a mesh axis runs over, the one named last changes fastest.
Arguments:
- positions: float32 [3, 64, 64, 128], P(None, ('tank', 'slab'), ('cross', 'sub')), parts along dimension 1, as said below
- velocities: float32 [3, 64, 64, 128], P(None, ('tank', 'slab'), ('cross', 'sub')), parts along dimension 1, may hold values from -6 to 6
- pair_i: int32 [8, 4, 1152], P(('tank', 'slab'), ('cross', 'sub')), parts along dimension 0, may hold values from 0 to 127, as said below
- pair_j: int32 [8, 4, 1152], P(('tank', 'slab'), ('cross', 'sub')), parts along dimension 0, may hold values from 0 to 179, as said below
- pair_count: int32 [8, 4], P(('tank', 'slab'), ('cross', 'sub')), parts along dimension 0, may hold values from 128 to 1152, as said below
- block_fill: int32 [64, 64], P(('tank', 'slab'), ('cross', 'sub')), parts along dimension 0, may hold values from 0 to 128, as said below
- block_body: int32 [64, 64], P(('tank', 'slab'), ('cross', 'sub')), parts along dimension 0, may hold values from 0 to 4
Outputs:
- density: float32 [64, 64, 128], P(('tank', 'slab'), ('cross', 'sub')), parts along dimension 0
- accel: float32 [3, 64, 64, 128], P(None, ('tank', 'slab'), ('cross', 'sub')), parts along dimension 1
- body_force: float32 [3, 8], P(None, 'tank'), parts along dimension 1
There are 2 independent parts, one for each index of `tank`. A program takes and returns all parts, laid end to end along the dimension named above; each array names one. Nothing has to cross between parts.
Inputs may be any that keep to these rules, and one draw needn't show every extreme that they name: `pair_i`: slots 0 to 127 of each row pair local block k with itself (extended block (k // 16 + 1) (18) + k % 16 + 1); the other slots pair each local block once with each of its eight neighbouring extended blocks, in a drawn order, those in which both blocks lie in the tank and have block_fill above 0 coming first. `pair_j`: see pair_i. pair_count is 128 plus the number of neighbour slots whose two blocks both lie in the tank and have block_fill above 0. `block_fill`: a block holds either no particles or 64 to 128. `block_body`: the value 4 marks a free fluid block. `positions`: particles of global block (a, b) have first coordinate in [2.6 a, 2.6 (a + 1)), second in [2.6 b, 2.6 (b + 1)) and third in [0, 18.9).
All inputs are finite; a program needn't handle non-finite values.
Results may differ from a plain program's by a relative error of at most 0.0003.
Values sent between devices are 32-bit elements; how exact they have to be, the bound alone decides.
A program may use at most 64 MiB of HBM per device.

v0:
```python
import math
import jax
import jax.numpy as jnp
from jax import lax
from jax.sharding import PartitionSpec as P

NBODY = 4
SMOOTH = 1.3
KERNEL_NORM = 21.0 / (16.0 * math.pi * SMOOTH**3)
SLOPE_NORM = 5.0 * KERNEL_NORM / SMOOTH**2
VISCOSITY = 0.2
GRAVITY = 1.0


def padded(shard, sides, width):
    for axis, dim in sides:
        devices, length = (lax.axis_size(axis), shard.shape[dim])
        up = [(i, (i + 1) % devices) for i in range(devices - 1)]
        down = [(j, i) for i, j in up]
        last = lax.slice_in_dim(shard, length - width, length, axis=dim)
        initial = lax.slice_in_dim(shard, 0, width, axis=dim)
        before = lax.ppermute(last, axis, up)
        after = lax.ppermute(initial, axis, down)
        shard = jnp.concatenate([before, shard, after], axis=dim)
    return shard


def pair_shape(first_tiles, second_tiles):
    offsets = first_tiles[:, 0:3, :, None] - second_tiles[:, 0:3, None, :]
    distance = jnp.sqrt(jnp.sum(offsets * offsets, axis=1)) / SMOOTH
    remain = jnp.maximum(1.0 - 0.5 * distance, 0.0)
    return (offsets, distance, remain)


def density_terms(first_tiles, second_tiles):
    offsets, distance, remain = pair_shape(first_tiles, second_tiles)
    kernel = KERNEL_NORM * remain**4 * (2.0 * distance + 1.0)
    return jnp.sum(kernel * second_tiles[:, 3, None, :], axis=2)


def force_terms(first_tiles, second_tiles):
    offsets, distance, remain = pair_shape(first_tiles, second_tiles)
    slope = SLOPE_NORM * remain**3 * second_tiles[:, 3, None, :]
    pushed = slope * (first_tiles[:, 7, :, None] + second_tiles[:, 7, None, :])
    push_sum = jnp.sum(pushed[:, None] * offsets, axis=3)
    drift = first_tiles[:, 4:7, :, None] - second_tiles[:, 4:7, None, :]
    drag_sum = jnp.sum(slope[:, None] * drift, axis=3)
    return push_sum - VISCOSITY * drag_sum


def tile_loop(
    begin_slot, end_slot, total_slots, group_size, fetch_tiles, kernel, store_values, initial
):
    first_group = begin_slot // group_size
    last_group = (end_slot + group_size - 1) // group_size

    def advance(group_index, carried):
        nominal = group_index * group_size
        anchor = jnp.minimum(nominal, total_slots - group_size).astype(jnp.int32)
        slot_ids = anchor + lax.broadcasted_iota(jnp.int32, (group_size,), 0)
        wanted = (slot_ids >= jnp.maximum(begin_slot, nominal)) & (
            slot_ids < jnp.minimum(end_slot, nominal + group_size)
        )
        first_tiles, second_tiles = fetch_tiles(anchor)
        values = kernel(first_tiles, second_tiles)
        weight = wanted.astype(jnp.float32).reshape((group_size,) + (1,) * (values.ndim - 1))
        return store_values(carried, anchor, values * weight)

    return lax.fori_loop(first_group, last_group, advance, initial)


def table_fetch(table, firsts, seconds, group_size):

    def fetch_tiles(anchor):
        first_ids = lax.dynamic_slice_in_dim(firsts, anchor, group_size)
        second_ids = lax.dynamic_slice_in_dim(seconds, anchor, group_size)
        return (jnp.take(table, first_ids, axis=0), jnp.take(table, second_ids, axis=0))

    return fetch_tiles


def scatter_store(targets, group_size):

    def store_values(carried, anchor, values):
        target_ids = lax.dynamic_slice_in_dim(targets, anchor, group_size)
        return carried.at[target_ids].add(values)

    return store_values


def shards(positions, velocities, pair_i, pair_j, pair_count, block_fill, block_body):
    lengthwise, columns = block_fill.shape
    local_count = lengthwise * columns
    frame_width = columns + 2
    slot_ids = lax.broadcasted_iota(jnp.int32, (lengthwise, columns, 128), 2)
    masses = (slot_ids < block_fill[:, :, None]).astype(jnp.float32)
    state = jnp.concatenate(
        [
            jnp.transpose(positions, (1, 2, 0, 3)),
            masses[:, :, None, :],
            jnp.transpose(velocities, (1, 2, 0, 3)),
        ],
        axis=2,
    )
    framed = padded(state, (("slab", 0), (("cross", "sub"), 1)), 1)
    table = framed.reshape((lengthwise + 2) * frame_width, 7, 128)
    local_firsts = pair_i.reshape(-1)
    ext_firsts = (local_firsts // columns + 1) * frame_width + local_firsts % columns + 1
    ext_seconds = pair_j.reshape(-1)
    total_slots = local_firsts.shape[0]
    live_count = pair_count.reshape(())
    group_size = min(16, 2 * local_count, total_slots)
    density_sums = tile_loop(
        0,
        live_count,
        total_slots,
        group_size,
        table_fetch(table, ext_firsts, ext_seconds, group_size),
        density_terms,
        scatter_store(local_firsts, group_size),
        jnp.zeros((local_count, 128), jnp.float32),
    )
    valid = masses.reshape(local_count, 128)
    density = density_sums * valid
    safe_density = jnp.where(valid > 0, density_sums, 1.0)
    pressure_term = valid * (safe_density**7 - 1.0) / (safe_density * safe_density)
    framed_pressure = padded(
        pressure_term.reshape(lengthwise, columns, 1, 128), (("slab", 0), (("cross", "sub"), 1)), 1
    )
    force_table = jnp.concatenate([table, framed_pressure.reshape(-1, 1, 128)], axis=1)
    hydro_start = jnp.zeros((local_count, 3, 128), jnp.float32)
    hydro = tile_loop(
        0,
        live_count,
        total_slots,
        group_size,
        table_fetch(force_table, ext_firsts, ext_seconds, group_size),
        force_terms,
        scatter_store(local_firsts, group_size),
        hydro_start,
    )
    hydro = hydro * valid[:, None, :]
    nothing = jnp.zeros_like(valid)
    gravity = jnp.stack([nothing, nothing, GRAVITY * valid], axis=1)
    accel = jnp.transpose((hydro - gravity).reshape(lengthwise, columns, 3, 128), (2, 0, 1, 3))
    block_sums = jnp.sum(hydro, axis=2)
    owners = (
        block_body.reshape(local_count)[:, None]
        == lax.broadcasted_iota(jnp.int32, (local_count, NBODY), 1)
    ).astype(jnp.float32)
    partial_force = jnp.dot(block_sums.T, owners, precision=lax.Precision.HIGHEST)
    totals = lax.psum(partial_force, ("slab", "cross", "sub"))
    slot_total = (
        128
        * lengthwise
        * lax.axis_size("slab")
        * columns
        * lax.axis_size("cross")
        * lax.axis_size("sub")
    )
    body_force = totals / math.sqrt(slot_total)
    return (density.reshape(lengthwise, columns, 128), accel, body_force)


def solution(mesh):
    placed = (
        P(None, ("tank", "slab"), ("cross", "sub"), None),
        P(None, ("tank", "slab"), ("cross", "sub"), None),
        P(("tank", "slab"), ("cross", "sub"), None),
        P(("tank", "slab"), ("cross", "sub"), None),
        P(("tank", "slab"), ("cross", "sub")),
        P(("tank", "slab"), ("cross", "sub")),
        P(("tank", "slab"), ("cross", "sub")),
    )
    return jax.shard_map(
        shards,
        mesh=mesh,
        in_specs=placed,
        out_specs=(
            P(("tank", "slab"), ("cross", "sub"), None),
            P(None, ("tank", "slab"), ("cross", "sub"), None),
            P(None, "tank"),
        ),
        check_vma=False,
    )
```

profile of v0, /device:TPU:0, one launch (start us, length us, event | category | flops | bytes accessed | tf_op | source)
XLA Modules:
  0.0 1040.7 jit_solution(2760082690979434666)
XLA Ops:
  2.3 4.9 collective-permute-start
  9.3 4.1 collective-permute-done.1
  17.8 2.7 collective-permute-done.3
  21.0 267.2 %while.24 = (s32[]{:T(128)}, f32[128,128]{1,0:T(8,128)S(1)}, s32[]{:T(128)}, s32[1152]{0:T(1024)S(1)}, s32[1152]{0:T(1024)S(1)}, /*index=5*/f32[180,7,128]{2,1,0...) while((s32[]{:T(128)}, f32[128,128]{1,0:T(8,128)S(1)}, ...), condition=%wide.region_4.6_spmd, body=%wide.region_0.5_spmd.sunk | while | flops 5005642 | bytes 2704879 | solution.py:69
  291.6 77.5 %collective-permute-done.5 = f32[1,16,1,128]{3,1,2,0:T(8,128)S(1)} collective-permute-done((f32[1,16,1,128]{3,1,2,0:T(8,128)S(1)}, f32[1,16,1,128]{3,1,2,0:T(8,128)S(1)}, u32[]{:S(2)}, u32[]{:S(2)}) %collective-permute-start.5) | collective-permute-done | bytes 8224 | tf_op jit(solution)/shard_map/ppermute | solution.py:23
  369.1 8.2 collective-permute-start.6
  378.9 2.1 collective-permute-done.7
  381.3 494.1 %while.25 = (s32[]{:T(128)}, f32[128,3,128]{2,1,0:T(4,128)S(1)}, s32[]{:T(128)}, s32[1152]{0:T(1024)S(1)}, s32[1152]{0:T(1024)S(1)}, /*index=5*/f32[180,8,128]{2...) while((s32[]{:T(128)}, f32[128,3,128]{2,1,0:T(4,128)S(1)}, ...), condition=%wide.region_10.13_spmd, body=%wide.region_5.12_spmd.sunk | while | flops 8962378 | bytes 7439471 | solution.py:69
  384.4 1.9 multiply_reduce_fusion.9
  393.2 1.9 multiply_reduce_fusion.9
  402.1 1.9 multiply_reduce_fusion.9
  410.9 1.9 multiply_reduce_fusion.9
  419.7 1.9 multiply_reduce_fusion.9
  428.5 1.9 multiply_reduce_fusion.9
  437.4 1.9 multiply_reduce_fusion.9
  446.2 1.9 multiply_reduce_fusion.9
  455.0 1.9 multiply_reduce_fusion.9
  463.8 1.9 multiply_reduce_fusion.9
  472.6 1.9 multiply_reduce_fusion.9
  481.5 1.9 multiply_reduce_fusion.9
  490.3 1.9 multiply_reduce_fusion.9
  499.1 1.9 multiply_reduce_fusion.9
  507.9 1.9 multiply_reduce_fusion.9
  516.8 1.9 multiply_reduce_fusion.9
  525.6 1.9 multiply_reduce_fusion.9
  534.4 1.9 multiply_reduce_fusion.9
  587.3 1.9 multiply_reduce_fusion.9
  605.0 1.9 multiply_reduce_fusion.9
  640.3 1.9 multiply_reduce_fusion.9
  737.3 1.9 multiply_reduce_fusion.9
  799.1 1.9 multiply_reduce_fusion.9
  876.6 163.5 %psum.7 = f32[3,4]{1,0:T(4,128)S(1)} all-reduce(f32[3,4]{1,0:T(4,128)S(1)} %fusion.12), channel_id=1, replica_groups=mesh['tank'=2,'slab'=4,'cross'=2,'sub'=2] {'slab','cross','sub'}, use_global_device_ids=true, to_apply=%region_12.15 | all-reduce | flops 12 | bytes 96 | tf_op jit(solution)/shard_map/psum | solution.py:152
  (1868 shorter events, 645.4 us)
Async XLA Ops:
  0.6 17.1 %copy-start.2 = (s32[8,16]{1,0:T(8,128)S(1)}, s32[8,16]{1,0:T(8,128)}, u32[]{:S(2)}) copy-start(s32[8,16]{1,0:T(8,128)} %param.20) | copy-start | bytes 1540
  0.6 19.9 %copy-start.1 = (f32[3,8,16,128]{3,2,1,0:T(8,128)S(1)}, f32[3,8,16,128]{3,2,1,0:T(8,128)}, u32[]{:S(2)}) copy-start(f32[3,8,16,128]{3,2,1,0:T(8,128)} %param.15) | copy-start | bytes 589828
  0.7 19.9 %copy-start = (f32[3,8,16,128]{3,2,1,0:T(8,128)S(1)}, f32[3,8,16,128]{3,2,1,0:T(8,128)}, u32[]{:S(2)}) copy-start(f32[3,8,16,128]{3,2,1,0:T(8,128)} %param.16) | copy-start | bytes 589828
  0.7 17.1 %copy-start.3 = (s32[1,1,1152]{2,1,0:T(1,128)S(1)}, s32[1,1,1152]{2,1,0:T(1,128)}, u32[]{:S(2)}) copy-start(s32[1,1,1152]{2,1,0:T(1,128)} %param.18) | copy-start | bytes 13828
  2.3 7.0 collective-permute-start
  7.3 6.1 collective-permute-start.1
  14.4 3.4 collective-permute-start.2
  15.7 4.8 collective-permute-start.3
  21.0 357.8 %copy-start.4 = (s32[8,16]{1,0:T(8,128)S(1)}, s32[8,16]{1,0:T(8,128)}, u32[]{:S(2)}) copy-start(s32[8,16]{1,0:T(8,128)} %param.21) | copy-start | bytes 1540
  288.9 2.7 collective-permute-start.4
  290.2 78.9 %collective-permute-start.5 = (f32[1,16,1,128]{3,1,2,0:T(8,128)S(1)}, f32[1,16,1,128]{3,1,2,0:T(8,128)S(1)}, u32[]{:S(2)}, u32[]{:S(2)}) collective-permute-start(f32[1,16,1,128]{3,1,2,0:T(8,128)S(1)} %get-tuple-element.279), channel_id=1, source_target_pairs={{4,0},{8,4},{12,8},{5,1},{9,5},{13,9},{6,2},{10,6},{14,10},{7,3},{... | collective-permute-start | bytes 24584 | tf_op jit(solution)/shard_map/ppermute | solution.py:23
  369.1 9.8 collective-permute-start.6
  377.3 3.7 collective-permute-start.7
where the time goes:
time: 1040 us
  other arithmetic  550 us (53%)
  blocking collectives  164 us (16%)
  local copies, waits for them, and re-layouts  131 us (13%)
  loops' own time  87.8 us (8%)
  waiting for transfers between devices  86.4 us (8%)
  starting transfers between devices  20.9 us (2%)
    psum x1, blocking collectives, shards(): totals = lax.psum(partial_force, ('slab', 'cross', 'sub'))  164 us
    reduce_sum x112, other arithmetic, pair_shape(): distance = jnp.sqrt(jnp.sum(offsets * offsets, axis=1)) / SMOOTH  116 us
    reduce_sum x56, other arithmetic, force_terms(): drag_sum = jnp.sum(slope[:, None] * drift, axis=3)  105 us
    reduce_sum x56, other arithmetic, force_terms(): push_sum = jnp.sum(pushed[:, None] * offsets, axis=3)  104 us
    scatter-add x112, other arithmetic, store_values(): return carried.at[target_ids].add(values)  104 us
    another operation x2, loops' own time, tile_loop(): return lax.fori_loop(first_group, last_group, advance, initial)  87.8 us
    ppermute x4, waiting for transfers between devices, padded(): after = lax.ppermute(initial, axis, down)  86.3 us
    gather x112, local copies, waits for them, and re-layouts, fetch_tiles(): jnp.take(table, second_ids, axis=0)  63.3 us
  transfers between devices with their start and end apart: 8, of which 4 were waited for; matrix products, arithmetic and copies ran while one was open for 0% of the time, Pallas kernels for 0%

commit v1 on v0

--- a/solution.py
+++ b/solution.py
@@ -149,7 +149,7 @@
         == lax.broadcasted_iota(jnp.int32, (local_count, NBODY), 1)
     ).astype(jnp.float32)
     partial_force = jnp.dot(block_sums.T, owners, precision=lax.Precision.HIGHEST)
-    totals = lax.psum(partial_force, ("slab", "cross", "sub"))
+    totals = jnp.sum(jax.lax.all_gather(partial_force, ("slab", "cross", "sub")), axis=0)
     slot_total = (
         128
         * lengthwise

time: 1040 us -> 1040 us (level)
    psum x1 -> x0, blocking collectives: 164 us -> none  [shards(): totals = lax.psum(partial_force, ('slab', 'cross', 'sub'))]
    all_gather x0 -> x1, blocking collectives: none -> 160 us  [shards(): jax.lax.all_gather(partial_force, ('slab', 'cross', 'sub'))]
where the time goes in v1:
time: 1040 us
  other arithmetic  550 us (53%)
  blocking collectives  160 us (15%)
  local copies, waits for them, and re-layouts  131 us (13%)
  loops' own time  87.8 us (8%)
  waiting for transfers between devices  86.4 us (8%)
  starting transfers between devices  20.9 us (2%)
    all_gather x1, blocking collectives, shards(): jax.lax.all_gather(partial_force, ('slab', 'cross', 'sub'))  160 us
    reduce_sum x112, other arithmetic, pair_shape(): distance = jnp.sqrt(jnp.sum(offsets * offsets, axis=1)) / SMOOTH  116 us
    reduce_sum x56, other arithmetic, force_terms(): drag_sum = jnp.sum(slope[:, None] * drift, axis=3)  105 us
    reduce_sum x56, other arithmetic, force_terms(): push_sum = jnp.sum(pushed[:, None] * offsets, axis=3)  104 us
    scatter-add x112, other arithmetic, store_values(): return carried.at[target_ids].add(values)  104 us
    another operation x2, loops' own time, tile_loop(): return lax.fori_loop(first_group, last_group, advance, initial)  87.8 us
    ppermute x4, waiting for transfers between devices, padded(): after = lax.ppermute(initial, axis, down)  86.3 us
    gather x112, local copies, waits for them, and re-layouts, fetch_tiles(): jnp.take(table, second_ids, axis=0)  63.3 us
  transfers between devices with their start and end apart: 8, of which 4 were waited for; matrix products, arithmetic and copies ran while one was open for 0% of the time, Pallas kernels for 0%

profile of v1, /device:TPU:0, one launch (start us, length us, event | category | flops | bytes accessed | tf_op | source)
XLA Modules:
  0.0 1036.9 jit_solution(16932009715573856771)
XLA Ops:
  2.3 4.9 collective-permute-start
  9.3 4.1 collective-permute-done.1
  17.8 2.7 collective-permute-done.3
  21.0 267.2 %while.24 = (s32[]{:T(128)}, f32[128,128]{1,0:T(8,128)S(1)}, s32[]{:T(128)}, s32[1152]{0:T(1024)S(1)}, s32[1152]{0:T(1024)S(1)}, /*index=5*/f32[180,7,128]{2,1,0...) while((s32[]{:T(128)}, f32[128,128]{1,0:T(8,128)S(1)}, ...), condition=%wide.region_4.6_spmd, body=%wide.region_0.5_spmd.sunk | while | flops 5005642 | bytes 2704879 | solution.py:69
  291.6 77.5 %collective-permute-done.5 = f32[1,16,1,128]{3,1,2,0:T(8,128)S(1)} collective-permute-done((f32[1,16,1,128]{3,1,2,0:T(8,128)S(1)}, f32[1,16,1,128]{3,1,2,0:T(8,128)S(1)}, u32[]{:S(2)}, u32[]{:S(2)}) %collective-permute-start.5) | collective-permute-done | bytes 8224 | tf_op jit(solution)/shard_map/ppermute | solution.py:23
  369.1 8.2 collective-permute-start.6
  378.9 2.1 collective-permute-done.7
  381.3 494.1 %while.25 = (s32[]{:T(128)}, f32[128,3,128]{2,1,0:T(4,128)S(1)}, s32[]{:T(128)}, s32[1152]{0:T(1024)S(1)}, s32[1152]{0:T(1024)S(1)}, /*index=5*/f32[180,8,128]{2...) while((s32[]{:T(128)}, f32[128,3,128]{2,1,0:T(4,128)S(1)}, ...), condition=%wide.region_10.13_spmd, body=%wide.region_5.12_spmd.sunk | while | flops 8962378 | bytes 7439471 | solution.py:69
  384.4 1.9 multiply_reduce_fusion.9
  393.2 1.9 multiply_reduce_fusion.9
  402.1 1.9 multiply_reduce_fusion.9
  410.9 1.9 multiply_reduce_fusion.9
  419.7 1.9 multiply_reduce_fusion.9
  428.5 1.9 multiply_reduce_fusion.9
  437.4 1.9 multiply_reduce_fusion.9
  446.2 1.9 multiply_reduce_fusion.9
  455.0 1.9 multiply_reduce_fusion.9
  463.8 1.9 multiply_reduce_fusion.9
  472.6 1.9 multiply_reduce_fusion.9
  481.5 1.9 multiply_reduce_fusion.9
  490.3 1.9 multiply_reduce_fusion.9
  499.1 1.9 multiply_reduce_fusion.9
  507.9 1.9 multiply_reduce_fusion.9
  516.8 1.9 multiply_reduce_fusion.9
  525.6 1.9 multiply_reduce_fusion.9
  534.4 1.9 multiply_reduce_fusion.9
  587.3 1.9 multiply_reduce_fusion.9
  605.0 1.9 multiply_reduce_fusion.9
  640.3 1.9 multiply_reduce_fusion.9
  737.3 1.9 multiply_reduce_fusion.9
  799.1 1.9 multiply_reduce_fusion.9
  876.5 159.7 %all-gather.1 = f32[16,3,4]{2,1,0:T(4,128)S(1)} all-gather(f32[1,3,4]{2,1,0:T(4,128)S(1)} %convolution_bitcast_fusion), channel_id=2, replica_groups=mesh['tank'=2,'slab'=4,'cross'=2,'sub'=2] {'slab','cross','sub'}, dimensions={0}, use_global_device_ids=true | all-gather | bytes 816 | tf_op jit(solution)/shard_map/all_gather | solution.py:152
  (1869 shorter events, 645.4 us)
Async XLA Ops:
  0.6 17.1 %copy-start.2 = (s32[8,16]{1,0:T(8,128)S(1)}, s32[8,16]{1,0:T(8,128)}, u32[]{:S(2)}) copy-start(s32[8,16]{1,0:T(8,128)} %param.20) | copy-start | bytes 1540
  0.6 19.9 %copy-start.1 = (f32[3,8,16,128]{3,2,1,0:T(8,128)S(1)}, f32[3,8,16,128]{3,2,1,0:T(8,128)}, u32[]{:S(2)}) copy-start(f32[3,8,16,128]{3,2,1,0:T(8,128)} %param.15) | copy-start | bytes 589828
  0.7 19.9 %copy-start = (f32[3,8,16,128]{3,2,1,0:T(8,128)S(1)}, f32[3,8,16,128]{3,2,1,0:T(8,128)}, u32[]{:S(2)}) copy-start(f32[3,8,16,128]{3,2,1,0:T(8,128)} %param.16) | copy-start | bytes 589828
  0.7 17.1 %copy-start.3 = (s32[1,1,1152]{2,1,0:T(1,128)S(1)}, s32[1,1,1152]{2,1,0:T(1,128)}, u32[]{:S(2)}) copy-start(s32[1,1,1152]{2,1,0:T(1,128)} %param.18) | copy-start | bytes 13828
  2.3 7.0 collective-permute-start
  7.3 6.1 collective-permute-start.1
  14.4 3.4 collective-permute-start.2
  15.7 4.8 collective-permute-start.3
  21.0 357.8 %copy-start.4 = (s32[8,16]{1,0:T(8,128)S(1)}, s32[8,16]{1,0:T(8,128)}, u32[]{:S(2)}) copy-start(s32[8,16]{1,0:T(8,128)} %param.21) | copy-start | bytes 1540
  288.9 2.7 collective-permute-start.4
  290.2 78.9 %collective-permute-start.5 = (f32[1,16,1,128]{3,1,2,0:T(8,128)S(1)}, f32[1,16,1,128]{3,1,2,0:T(8,128)S(1)}, u32[]{:S(2)}, u32[]{:S(2)}) collective-permute-start(f32[1,16,1,128]{3,1,2,0:T(8,128)S(1)} %get-tuple-element.279), channel_id=1, source_target_pairs={{4,0},{8,4},{12,8},{5,1},{9,5},{13,9},{6,2},{10,6},{14,10},{7,3},{... | collective-permute-start | bytes 24584 | tf_op jit(solution)/shard_map/ppermute | solution.py:23
  369.1 9.8 collective-permute-start.6
  377.3 3.7 collective-permute-start.7
